TPU v7x, 512 devices: a whole 4x8x8 slice. The times are simulated.
512 devices in a mesh: seq: 8 (over y_hi, x), expert: 64 (over z, y_lo, core).
Axes of the slice: x: 4, y: 8 (y_hi: 2, y_lo: 4; y = y_hi * 4 + y_lo), z: 8, core: 2. Of those that a mesh axis runs over, the one named last changes fastest.
Arguments:
- hidden_in: bfloat16 [3072, 4096], P('seq', 'expert'), may hold values from -6 to 6
- queries: bfloat16 [3072, 8192], P('seq', 'expert'), may hold values from -150 to 150
- frame_keys: bfloat16 [24, 201, 1024], P('seq'), may hold values from -6 to 6
- frame_values: bfloat16 [24, 201, 1024], P('seq'), may hold values from -6 to 6
- cited_frame: int32 [3072], P('seq'), may hold values from 0 to 23, as said below
- frame_slot: int32 [24], replicated, may hold values from 0 to 23, as said below
- attn_gate: float32 [4096], P('expert'), may hold values from 0.3 to 2
- out_weight: bfloat16 [8192, 4096], P(None, 'expert'), may hold values from -0.0625 to 0.0625
- mlp_gain: float32 [4096], replicated, may hold values from 0.1 to 1.9
- expert_ids: int32 [3072, 2], P('seq'), may hold values from 0 to 63, all different within a row; in each aligned block of 384 rows (0 to 383, 384 to 767, ...) at most 36 rows name the same one
- gate_fixed: int32 [3072, 2], P('seq'), may hold values from 6554 to 65535
- w_in: bfloat16 [64, 4096, 2, 1024], P('expert', None, None, 'seq'), may hold values from -0.09375 to 0.09375
- w_down: bfloat16 [64, 1024, 4096], P('expert', 'seq'), may hold values from -0.1875 to 0.1875
Outputs:
- hidden_out: bfloat16 [3072, 4096], P('seq', 'expert')
Inputs may be any that keep to these rules, and one draw needn't show every extreme that they name: `cited_frame`: any token may cite any frame. `frame_slot`: A permutation of the frame ids. `expert_ids`: the two experts of a token differ; among the 384 tokens of one seq shard no expert is named more than 36 times.
All inputs are finite; a program needn't handle non-finite values.
Results may differ from a plain program's by a relative error of at most 0.015.
Values may be sent and summed in bfloat16 or wider, within the bound.
No kernel may reach another device: no remote copies, remote signals or barrier semaphores. Data moves between devices by JAX's collectives and lax.ppermute only.
A program may use at most 64 MiB of HBM per device.

v0:
```python
import math
import jax
import jax.numpy as jnp
from jax import lax
from jax.sharding import Mesh
from jax.sharding import PartitionSpec as P

FIXED_SCALE = 1.0 / 65536.0
NORM_EPSILON = 1e-05
MASKED_SCORE = -1e30
SEQ = ("yh", "x")
EXP = ("z", "yl", "core")
NEAR = ("yl", "core")
BOTH = ("yh",) + EXP
f32, bf16 = (jnp.float32, jnp.bfloat16)


def swap(v, axis):
    return lax.ppermute(v, axis, [(0, 1), (1, 0)])


def shift(v, axis, by):
    n = lax.axis_size(axis)
    return lax.ppermute(v, axis, [(i, (i + by) % n) for i in range(n)])


def tie(*values):
    return lax.optimization_barrier(values)


def route_tables(expert_ids, gate_fixed, experts, capacity):
    token_count, top_count = expert_ids.shape
    flat_ids = expert_ids.reshape(-1)
    assigned = flat_ids.shape[0]
    expert_cols = lax.broadcasted_iota(jnp.int32, (assigned, experts), 1)
    matches = flat_ids[:, None] == expert_cols
    before = lax.broadcasted_iota(jnp.int32, (assigned, assigned), 1) < lax.broadcasted_iota(
        jnp.int32, (assigned, assigned), 0
    )
    counts = jnp.dot(before.astype(bf16), matches.astype(bf16), preferred_element_type=f32)
    rank_of = jnp.sum(jnp.where(matches, counts, 0.0), axis=1).astype(jnp.int32)
    slot_of = (flat_ids * capacity + rank_of).reshape(token_count, top_count)
    slot_cols = lax.broadcasted_iota(jnp.int32, (token_count, experts * capacity), 1)
    selectors = [slot_of[:, k : k + 1] == slot_cols for k in range(top_count)]
    weights = gate_fixed.astype(f32) * FIXED_SCALE
    return (selectors, weights)


def attention(queries, keys, values, local_frame, frame_rows):
    width = keys.shape[0]
    scale = 1.0 / math.sqrt(queries.shape[1])
    scores = (
        lax.dot_general(queries, keys, (((1,), (1,)), ((), ())), preferred_element_type=f32) * scale
    )
    column_frame = lax.broadcasted_iota(jnp.int32, (1, width), 1) // frame_rows
    inside = column_frame == local_frame[:, None]
    scores = jnp.where(inside, scores, MASKED_SCORE)
    row_max = jnp.max(scores, axis=1, keepdims=True)
    expon = jnp.exp(scores - row_max)
    row_total = jnp.sum(expon, axis=1, keepdims=True)
    probability = (expon / row_total).astype(bf16)
    mixed = jnp.dot(probability, values, preferred_element_type=f32)
    return jnp.where(local_frame[:, None] >= 0, mixed, 0.0).astype(bf16)


def per_device(
    hidden_in,
    queries,
    frame_keys,
    frame_values,
    cited_frame,
    frame_slot,
    attn_gate,
    out_weight,
    mlp_gain,
    expert_ids,
    gate_fixed,
    w_in,
    w_down,
):
    head = queries.shape[1]
    tokens = queries.shape[0]
    nx, nz, nh = (lax.axis_size("x"), lax.axis_size("z"), lax.axis_size("yh"))
    experts = lax.axis_size(EXP)
    near = lax.axis_size(NEAR)
    feats = hidden_in.shape[1]
    yh, x, z = (lax.axis_index("yh"), lax.axis_index("x"), lax.axis_index("z"))
    held, frame_rows = (frame_keys.shape[0], frame_keys.shape[1])
    own = jnp.concatenate(
        [
            lax.dynamic_slice_in_dim(frame_keys, z * head, head, 2).reshape(
                held * frame_rows, head
            ),
            lax.dynamic_slice_in_dim(frame_values, z * head, head, 2).reshape(
                held * frame_rows, head
            ),
        ],
        axis=0,
    )
    other = swap(own, "yh")
    half = held * frame_rows
    keys = jnp.concatenate([own[:half], other[:half]], axis=0)
    values = jnp.concatenate([own[half:], other[half:]], axis=0)
    frame_cols = lax.broadcasted_iota(jnp.int32, (tokens, frame_slot.shape[0]), 1)
    token_slot = jnp.sum(
        jnp.where(cited_frame[:, None] == frame_cols, frame_slot[None, :], 0), axis=1
    )
    slot_rows = (
        jnp.zeros((16, head), bf16)
        .at[: tokens // head]
        .set(token_slot.reshape(tokens // head, head).astype(bf16))
    )
    packed = jnp.concatenate([queries, slot_rows])
    gathered = jnp.stack([packed] + [shift(packed, "x", k) for k in range(1, nx)])
    turned = out_weight.T.reshape(feats, nz, near * head).transpose(1, 0, 2)
    near_weight = lax.all_to_all(turned, "z", 0, 0, tiled=True).reshape(nz * feats, near * head)
    in_rows = jnp.concatenate([w_in[0, :, 0], w_in[0, :, 1]], axis=0)
    in_all = lax.all_gather(in_rows, "x")
    down_all = lax.all_gather(w_down[0], "x", tiled=True)
    all_queries = gathered[:, :tokens].reshape(nx * tokens, head)
    all_slots = gathered[:, tokens : tokens + tokens // head].reshape(nx * tokens).astype(jnp.int32)
    own_frame = all_slots - held * (yh * nx + x)
    other_frame = all_slots - held * ((1 - yh) * nx + x)
    local_frame = jnp.where(
        (own_frame >= 0) & (own_frame < held),
        own_frame,
        jnp.where((other_frame >= 0) & (other_frame < held), other_frame + held, -1),
    )
    mixed = attention(all_queries, keys, values, local_frame, frame_rows)
    back = mixed.reshape(nx, tokens, head)
    attended = sum(
        ((shift(back[k], "x", -k) if k else back[k]).astype(f32) for k in range(nx))
    ).astype(bf16)
    heads = lax.all_gather(attended, NEAR, axis=1, tiled=True)
    partial = lax.dot_general(
        near_weight, heads, (((1,), (1,)), ((), ())), preferred_element_type=f32
    ).astype(bf16)
    parts = lax.all_to_all(partial.reshape(nz, feats, tokens), "z", 0, 0, tiled=True)
    projected = jnp.sum(parts.astype(f32), axis=0)
    mid = (hidden_in.T.astype(f32) + jnp.tanh(attn_gate)[:, None] * projected).astype(bf16)
    capacity = 6 * tokens // experts
    selectors, weights = route_tables(expert_ids, gate_fixed, experts, capacity)
    select_rows = (selectors[0] | selectors[1]).astype(bf16)
    sent = lax.dot_general(
        select_rows, mid, (((0,), (1,)), ((), ())), preferred_element_type=f32
    ).astype(bf16)
    sent = jnp.broadcast_to(
        sent.reshape(1, experts, capacity, feats), (nh, experts, capacity, feats)
    )
    came = lax.all_to_all(sent.reshape(-1, capacity, feats), BOTH, 0, 0, tiled=True)
    rows = came.reshape(nh, experts, capacity, feats).transpose(0, 2, 1, 3)
    (rows,) = tie(rows.reshape(nh * capacity, experts * feats))
    wide = rows.astype(f32)
    mean_square = jnp.mean(wide * wide, axis=1, keepdims=True)
    normed = (wide * lax.rsqrt(mean_square + NORM_EPSILON) * mlp_gain).astype(bf16)
    width = w_in.shape[1]

    def gated(weight):
        gate = jnp.dot(normed, weight[:width], preferred_element_type=f32)
        up = jnp.dot(normed, weight[width:], preferred_element_type=f32)
        return (jax.nn.silu(gate) * up).astype(bf16)

    act = jnp.concatenate([gated(in_all[k]) for k in range(nx)], axis=1)
    down = jnp.dot(act, down_all, preferred_element_type=f32)
    (down,) = tie(down.astype(bf16))
    dealt = (
        down.reshape(nh, capacity, experts, feats)
        .transpose(0, 2, 1, 3)
        .reshape(-1, capacity, feats)
    )
    back_sums = lax.all_to_all(dealt, BOTH, 0, 0, tiled=True)
    back_sums = back_sums.reshape(nh, experts * capacity, feats).astype(f32)
    came_back = jnp.sum(back_sums, axis=0).astype(bf16)
    mixed_out = sum(
        (
            jnp.dot(s.astype(bf16), came_back, preferred_element_type=f32) * weights[:, k : k + 1]
            for k, s in enumerate(selectors)
        )
    )
    return (mid.T.astype(f32) + mixed_out).astype(bf16)


def solution(mesh):
    fine = Mesh(mesh.devices.reshape(2, 4, 8, 4, 2), SEQ + EXP)
    return jax.shard_map(
        per_device,
        mesh=fine,
        in_specs=(
            P(SEQ, EXP),
            P(SEQ, EXP),
            P(SEQ, None, None),
            P(SEQ, None, None),
            P(SEQ),
            P(),
            P(EXP),
            P(None, EXP),
            P(),
            P(SEQ, None),
            P(SEQ, None),
            P(EXP, None, None, SEQ),
            P(EXP, SEQ, None),
        ),
        out_specs=P(SEQ, EXP),
        check_vma=False,
    )
```

profile of v0, /device:TPU:1, one launch (start us, length us, event | category | flops | bytes accessed | tf_op | source)
XLA Modules:
  0.0 229.7 jit_solution(6140297716444577920)
XLA Ops:
  6.5 5.7 %fusion.77 = (bf16[1,4096,1,128]{3,2,1,0:T(2,128)(2,1)S(1)}, bf16[1,4096,1,128]{3,2,1,0:T(2,128)(2,1)S(1)}) fusion(bf16[1,4096,2,128]{3,2,1,0:T(2,128)(2,1)} %param.26), kind=kLoop, calls=%fused_computation.122 | loop fusion | bytes 4194304 | tf_op jit(solution)/shard_map/slice | solution.py:117
  15.6 3.9 %collective-permute-start = (bf16[400,128]{1,0:T(8,128)(2,1)}, bf16[400,128]{1,0:T(8,128)(2,1)S(1)}, u32[]{:S(2)}, u32[]{:S(2)}) collective-permute-start(bf16[400,128]{1,0:T(8,128)(2,1)} %get-tuple-element.33), channel_id=1, source_target_pairs={{0,64},{64,128},{128,192},{192,0},{1,65},{65,129},{129,193},{193,1... | collective-permute-start | bytes 307208 | tf_op jit(solution)/shard_map/ppermute | solution.py:24
  19.5 4.4 %collective-permute-start.1 = (bf16[400,128]{1,0:T(8,128)(2,1)}, bf16[400,128]{1,0:T(8,128)(2,1)S(1)}, u32[]{:S(2)}, u32[]{:S(2)}) collective-permute-start(bf16[400,128]{1,0:T(8,128)(2,1)} %get-tuple-element.33), channel_id=1, source_target_pairs={{0,128},{64,192},{128,0},{192,64},{1,129},{65,193},{129,1},{193,65... | collective-permute-start | bytes 307208 | tf_op jit(solution)/shard_map/ppermute | solution.py:24
  23.9 3.1 %collective-permute-start.2 = (bf16[400,128]{1,0:T(8,128)(2,1)}, bf16[400,128]{1,0:T(8,128)(2,1)S(1)}, u32[]{:S(2)}, u32[]{:S(2)}) collective-permute-start(bf16[400,128]{1,0:T(8,128)(2,1)} %get-tuple-element.33), channel_id=1, source_target_pairs={{0,192},{64,0},{128,64},{192,128},{1,193},{65,1},{129,65},{193,129... | collective-permute-start | bytes 307208 | tf_op jit(solution)/shard_map/ppermute | solution.py:24
  28.9 7.4 %collective-permute-start.3 = (bf16[1206,128]{1,0:T(8,128)(2,1)}, bf16[1206,128]{1,0:T(8,128)(2,1)S(1)}, u32[]{:S(2)}, u32[]{:S(2)}) collective-permute-start(bf16[1206,128]{1,0:T(8,128)(2,1)} %pad_maximum_fusion.4), channel_id=1, source_target_pairs={{0,256},{256,0},{1,257},{257,1},{2,258},{258,2},{3,259},{259,3},{4... | collective-permute-start | bytes 926216 | tf_op jit(solution)/shard_map/ppermute | solution.py:19
  38.5 10.0 %all-to-all-start = ((bf16[8,64,1024]{2,1,0:T(8,128)(2,1)}), bf16[8,64,1024]{2,1,0:T(8,128)(2,1)S(1)}, u32[]{:S(2)}, u32[]{:S(2)}) async-start(bf16[8,64,1024]{2,1,0:T(8,128)(2,1)} %copy.61), calls=%async_computation | async-start | bytes 2097152 | tf_op jit(solution)/shard_map/all_to_all | solution.py:116
  55.3 4.0 %collective-permute-start.5 = (bf16[384,128]{1,0:T(8,128)(2,1)S(1)}, bf16[384,128]{1,0:T(8,128)(2,1)S(1)}, u32[]{:S(2)}, u32[]{:S(2)}) collective-permute-start(bf16[384,128]{1,0:T(8,128)(2,1)S(1)} %get-tuple-element.29), channel_id=1, source_target_pairs={{0,128},{64,192},{128,0},{192,64},{1,129},{65,193},{129,1},{193,65... | collective-permute-start | bytes 294920 | tf_op jit(solution)/shard_map/ppermute | solution.py:24
  59.3 1.9 collective-permute-start.6
  61.4 3.3 %collective-permute-done.5 = bf16[384,128]{1,0:T(8,128)(2,1)S(1)} collective-permute-done((bf16[384,128]{1,0:T(8,128)(2,1)S(1)}, bf16[384,128]{1,0:T(8,128)(2,1)S(1)}, u32[]{:S(2)}, u32[]{:S(2)}) %collective-permute-start.5) | collective-permute-done | bytes 98336 | tf_op jit(solution)/shard_map/ppermute | solution.py:24
  64.8 4.6 %collective-permute-done.6 = bf16[384,128]{1,0:T(8,128)(2,1)S(1)} collective-permute-done((bf16[384,128]{1,0:T(8,128)(2,1)S(1)}, bf16[384,128]{1,0:T(8,128)(2,1)S(1)}, u32[]{:S(2)}, u32[]{:S(2)}) %collective-permute-start.6) | collective-permute-done | bytes 98336 | tf_op jit(solution)/shard_map/ppermute | solution.py:24
  69.4 17.5 %all_gather.12 = bf16[384,1024]{1,0:T(8,128)(2,1)S(1)} all-gather(bf16[384,128]{1,0:T(8,128)(2,1)S(1)} %add_convert_fusion), channel_id=1, replica_groups=mesh['yh'=2,'x'=4,'z'=8,'yl'=4,'core'=2] {'yl','core'}, dimensions={1}, use_global_device_ids=true | all-gather | bytes 884736 | tf_op jit(solution)/shard_map/all_gather | solution.py:134
  88.5 10.1 %all-to-all-start.1 = ((bf16[8,64,384]{2,1,0:T(8,128)(2,1)}), bf16[8,64,384]{2,1,0:T(8,128)(2,1)S(1)}, u32[]{:S(2)}, u32[]{:S(2)}) async-start(bf16[8,64,384]{2,1,0:T(8,128)(2,1)} %bitcast.10), calls=%async_computation.1 | async-start | bytes 786432 | tf_op jit(solution)/shard_map/all_to_all | solution.py:138
  99.7 14.1 %all-to-all-done.1 = bf16[8,64,384]{2,1,0:T(8,128)(2,1)S(1)} async-done(((bf16[8,64,384]{2,1,0:T(8,128)(2,1)}), bf16[8,64,384]{2,1,0:T(8,128)(2,1)S(1)}, u32[]{:S(2)}, u32[]{:S(2)}) %all-to-all-start.1) | async-done | bytes 393248 | tf_op jit(solution)/shard_map/all_to_all | solution.py:138
  116.4 29.2 %all_to_all.20 = bf16[128,2,1152]{2,1,0:T(2,128)(2,1)} all-to-all(bf16[128,2,1152]{2,1,0:T(2,128)(2,1)S(1)} %reshape.179), channel_id=1, replica_groups=mesh['yh'=2,'x'=4,'z'=8,'yl'=4,'core'=2] {'yh','z','yl','core'}, dimensions={0} | all-to-all | bytes 1179648 | tf_op jit(solution)/shard_map/all_to_all | solution.py:150
  145.7 2.7 %reshape.180 = bf16[128,36,64]{2,1,0:T(8,128)(2,1)S(1)} reshape(bf16[128,2,1152]{2,1,0:T(2,128)(2,1)} %all_to_all.20) | data formatting | bytes 1179648
  148.4 2.9 %copy.72 = bf16[2,64,36,64]{1,0,3,2:T(2,128)(2,1)} copy(bf16[2,64,36,64]{3,2,1,0:T(8,128)(2,1)S(1)} %bitcast.72) | data formatting | bytes 1179648 | tf_op jit(solution)/shard_map/reshape | solution.py:151
  151.3 2.6 %copy.67 = bf16[2,36,64,64]{3,2,1,0:T(8,128)(2,1)S(1)} copy(bf16[2,36,64,64]{2,0,3,1:T(2,128)(2,1)} %bitcast.75) | data formatting | bytes 1179648 | tf_op jit(solution)/shard_map/transpose | solution.py:151
  156.9 2.0 fusion.36
  163.8 5.4 %all-gather.7.cloned.1.call-done = bf16[1,512,4096]{2,1,0:T(8,128)(2,1)} async-done(((bf16[1,128,4096]{2,1,0:T(8,128)(2,1)}), bf16[1,512,4096]{2,1,0:T(8,128)(2,1)}) %all-gather.7.cloned.1.call-update) | async-done | bytes 4194320 | tf_op jit(solution)/shard_map/all_gather | solution.py:119
  169.1 3.0 %convolution_convert_fusion = bf16[72,4096]{1,0:T(8,128)(2,1)S(1)} fusion(bf16[1,512,4096]{2,1,0:T(8,128)(2,1)} %all-gather.7.cloned.1.call-done, bf16[72,128]{1,0:T(8,128)(2,1)S(1)} %fusion.33, bf16[72,128]{1,0:T(8,128)(2,1)S(1)} %fusion.32, bf16[72,128]{1,0:T(8,128)(2,1)S(1)} %fusion.31, bf16[72,128]{1,0:T(8,128)(2,1)S(1)} %fusion.30), kind=kOutput, calls=%fused_computation.5 | convolution fusion | flops 302579712 | bytes 4857856 | tf_op jit(solution)/shard_map/dot_general | solution.py:164
  173.4 2.1 copy.70
  175.5 3.6 %copy.73 = bf16[2,64,36,64]{3,2,1,0:T(8,128)(2,1)S(1)} copy(bf16[2,64,36,64]{1,0,3,2:T(2,128)(2,1)} %bitcast.76) | data formatting | bytes 1179648 | tf_op jit(solution)/shard_map/reshape | solution.py:169
  180.7 14.3 %all-to-all-start.3 = ((bf16[128,2,1152]{2,1,0:T(2,128)(2,1)}), bf16[128,2,1152]{2,1,0:T(2,128)(2,1)S(1)}, u32[]{:S(2)}, u32[]{:S(2)}) async-start(bf16[128,2,1152]{2,1,0:T(2,128)(2,1)} %reshape.181), calls=%async_computation.3 | async-start | bytes 1179648 | tf_op jit(solution)/shard_map/all_to_all | solution.py:171
  195.1 21.0 %all-to-all-done.3 = bf16[128,2,1152]{2,1,0:T(2,128)(2,1)S(1)} async-done(((bf16[128,2,1152]{2,1,0:T(2,128)(2,1)}), bf16[128,2,1152]{2,1,0:T(2,128)(2,1)S(1)}, u32[]{:S(2)}, u32[]{:S(2)}) %all-to-all-start.3) | async-done | bytes 589856 | tf_op jit(solution)/shard_map/all_to_all | solution.py:171
  (97 shorter events, 36.6 us)
Async XLA Ops:
  6.5 20.4 %copy-start = (bf16[3,201,1024]{2,1,0:T(8,128)(2,1)S(1)}, bf16[3,201,1024]{2,1,0:T(8,128)(2,1)}, u32[]{:S(2)}) copy-start(bf16[3,201,1024]{2,1,0:T(8,128)(2,1)} %param.17) | copy-start | bytes 3704836
  6.5 148.5 %all-gather.5.cloned.1.call-start = ((), (), s32[]{:S(2)}) async-start(), calls=%async_computation.4 | async-start | bytes 10485760 | tf_op jit(solution)/shard_map/all_gather | solution.py:118
  14.0 0.7 copy-start.5
  14.0 0.7 copy-start.6
  14.0 0.9 copy-start.2
  14.0 22.3 %copy-start.1 = (bf16[8192,64]{0,1:T(8,128)(2,1)S(1)}, bf16[8192,64]{0,1:T(8,128)(2,1)}, u32[]{:S(2)}) copy-start(bf16[8192,64]{0,1:T(8,128)(2,1)} %param.22) | copy-start | bytes 3145732
  15.6 33.7 %collective-permute-start = (bf16[400,128]{1,0:T(8,128)(2,1)}, bf16[400,128]{1,0:T(8,128)(2,1)S(1)}, u32[]{:S(2)}, u32[]{:S(2)}) collective-permute-start(bf16[400,128]{1,0:T(8,128)(2,1)} %get-tuple-element.33), channel_id=1, source_target_pairs={{0,64},{64,128},{128,192},{192,0},{1,65},{65,129},{129,193},{193,1... | collective-permute-start | bytes 307208 | tf_op jit(solution)/shard_map/ppermute | solution.py:24
  19.5 29.8 %collective-permute-start.1 = (bf16[400,128]{1,0:T(8,128)(2,1)}, bf16[400,128]{1,0:T(8,128)(2,1)S(1)}, u32[]{:S(2)}, u32[]{:S(2)}) collective-permute-start(bf16[400,128]{1,0:T(8,128)(2,1)} %get-tuple-element.33), channel_id=1, source_target_pairs={{0,128},{64,192},{128,0},{192,64},{1,129},{65,193},{129,1},{193,65... | collective-permute-start | bytes 307208 | tf_op jit(solution)/shard_map/ppermute | solution.py:24
  23.9 25.4 %collective-permute-start.2 = (bf16[400,128]{1,0:T(8,128)(2,1)}, bf16[400,128]{1,0:T(8,128)(2,1)S(1)}, u32[]{:S(2)}, u32[]{:S(2)}) collective-permute-start(bf16[400,128]{1,0:T(8,128)(2,1)} %get-tuple-element.33), channel_id=1, source_target_pairs={{0,192},{64,0},{128,64},{192,128},{1,193},{65,1},{129,65},{193,129... | collective-permute-start | bytes 307208 | tf_op jit(solution)/shard_map/ppermute | solution.py:24
  28.9 20.6 %collective-permute-start.3 = (bf16[1206,128]{1,0:T(8,128)(2,1)}, bf16[1206,128]{1,0:T(8,128)(2,1)S(1)}, u32[]{:S(2)}, u32[]{:S(2)}) collective-permute-start(bf16[1206,128]{1,0:T(8,128)(2,1)} %pad_maximum_fusion.4), channel_id=1, source_target_pairs={{0,256},{256,0},{1,257},{257,1},{2,258},{258,2},{3,259},{259,3},{4... | collective-permute-start | bytes 926216 | tf_op jit(solution)/shard_map/ppermute | solution.py:19
  38.5 48.5 %all-to-all-start = ((bf16[8,64,1024]{2,1,0:T(8,128)(2,1)}), bf16[8,64,1024]{2,1,0:T(8,128)(2,1)S(1)}, u32[]{:S(2)}, u32[]{:S(2)}) async-start(bf16[8,64,1024]{2,1,0:T(8,128)(2,1)} %copy.61), calls=%async_computation | async-start | bytes 2097152 | tf_op jit(solution)/shard_map/all_to_all | solution.py:116
  48.5 120.6 %all-gather.7.cloned.1.call-start = ((), (), s32[]{:S(2)}) async-start(), calls=%async_computation.5 | async-start | bytes 5242880 | tf_op jit(solution)/shard_map/all_gather | solution.py:119
  53.4 8.0 %collective-permute-start.4 = (bf16[384,128]{1,0:T(8,128)(2,1)S(1)}, bf16[384,128]{1,0:T(8,128)(2,1)S(1)}, u32[]{:S(2)}, u32[]{:S(2)}) collective-permute-start(bf16[384,128]{1,0:T(8,128)(2,1)S(1)} %get-tuple-element.27), channel_id=1, source_target_pairs={{0,192},{64,0},{128,64},{192,128},{1,193},{65,1},{129,65},{193,129... | collective-permute-start | bytes 294920 | tf_op jit(solution)/shard_map/ppermute | solution.py:24
  55.3 9.4 %collective-permute-start.5 = (bf16[384,128]{1,0:T(8,128)(2,1)S(1)}, bf16[384,128]{1,0:T(8,128)(2,1)S(1)}, u32[]{:S(2)}, u32[]{:S(2)}) collective-permute-start(bf16[384,128]{1,0:T(8,128)(2,1)S(1)} %get-tuple-element.29), channel_id=1, source_target_pairs={{0,128},{64,192},{128,0},{192,64},{1,129},{65,193},{129,1},{193,65... | collective-permute-start | bytes 294920 | tf_op jit(solution)/shard_map/ppermute | solution.py:24
  59.3 10.0 %collective-permute-start.6 = (bf16[384,128]{1,0:T(8,128)(2,1)S(1)}, bf16[384,128]{1,0:T(8,128)(2,1)S(1)}, u32[]{:S(2)}, u32[]{:S(2)}) collective-permute-start(bf16[384,128]{1,0:T(8,128)(2,1)S(1)} %get-tuple-element.28), channel_id=1, source_target_pairs={{0,64},{64,128},{128,192},{192,0},{1,65},{65,129},{129,193},{193,1... | collective-permute-start | bytes 294920 | tf_op jit(solution)/shard_map/ppermute | solution.py:24
  87.0 11.7 %copy-start.3 = (s32[384,2]{0,1:T(2,128)S(1)}, s32[384,2]{0,1:T(2,128)}, u32[]{:S(2)}) copy-start(s32[384,2]{0,1:T(2,128)} %param.24) | copy-start | bytes 9220
  87.6 12.0 %copy-start.11 = (f32[64]{0:T(128)S(1)}, f32[64]{0:T(128)}, u32[]{:S(2)}) copy-start(f32[64]{0:T(128)} %param.21) | copy-start | bytes 772
  87.6 26.3 %copy-start.8 = (bf16[384,64]{0,1:T(8,128)(2,1)S(1)}, bf16[384,64]{0,1:T(8,128)(2,1)}, u32[]{:S(2)}) copy-start(bf16[384,64]{0,1:T(8,128)(2,1)} %param.15) | copy-start | bytes 147460
  88.5 25.3 %all-to-all-start.1 = ((bf16[8,64,384]{2,1,0:T(8,128)(2,1)}), bf16[8,64,384]{2,1,0:T(8,128)(2,1)S(1)}, u32[]{:S(2)}, u32[]{:S(2)}) async-start(bf16[8,64,384]{2,1,0:T(8,128)(2,1)} %bitcast.10), calls=%async_computation.1 | async-start | bytes 786432 | tf_op jit(solution)/shard_map/all_to_all | solution.py:138
  151.3 3.8 %copy-start.10 = (f32[4096]{0:T(1024)S(1)}, f32[4096]{0:T(1024)}, u32[]{:S(2)}) copy-start(f32[4096]{0:T(1024)} %param.23) | copy-start | bytes 49156
  155.1 7.1 %copy-start.7 = (bf16[32768,128]{1,0:T(8,128)(2,1)S(1)}, bf16[32768,128]{1,0:T(8,128)(2,1)}, u32[]{:S(2)}) copy-start(bf16[32768,128]{1,0:T(8,128)(2,1)} %all-gather.5.cloned.1.call-done) | copy-start | bytes 25165828
  179.2 15.9 %copy-start.4 = (s32[384,2]{0,1:T(2,128)S(1)}, s32[384,2]{0,1:T(2,128)}, u32[]{:S(2)}) copy-start(s32[384,2]{0,1:T(2,128)} %param.25) | copy-start | bytes 9220
  180.7 35.4 %all-to-all-start.3 = ((bf16[128,2,1152]{2,1,0:T(2,128)(2,1)}), bf16[128,2,1152]{2,1,0:T(2,128)(2,1)S(1)}, u32[]{:S(2)}, u32[]{:S(2)}) async-start(bf16[128,2,1152]{2,1,0:T(2,128)(2,1)} %reshape.181), calls=%async_computation.3 | async-start | bytes 1179648 | tf_op jit(solution)/shard_map/all_to_all | solution.py:171
  218.5 2.8 %copy-start.9 = (bf16[384,64]{0,1:T(8,128)(2,1)S(1)}, bf16[384,64]{0,1:T(8,128)(2,1)}, u32[]{:S(2)}) copy-start(bf16[384,64]{0,1:T(8,128)(2,1)} %param.15) | copy-start | bytes 147460
Sparse Core Ops, SparseCore 0:
  14.2 98.1 all-gather.4
  114.5 54.5 all-gather.6
where the time goes:
time: 231 us; the launch traced here: 230 us
  starting transfers between devices  61.1 us (26%)
  waiting for transfers between devices  49.4 us (21%)
  blocking collectives  46.7 us (20%)
  local copies, waits for them, and re-layouts  33.2 us (14%)
  matrix products  19 us (8%)
  between operations  14 us (6%)
  other arithmetic  6.39 us (3%)
    all_to_all x1, blocking collectives, per_device(): lax.all_to_all(sent.reshape(-1, capacity, feats), BOTH, 0, 0, tiled=True)  29.2 us
    all_to_all x1, waiting for transfers between devices, per_device(): back_sums = lax.all_to_all(dealt, BOTH, 0, 0, tiled=True)  21 us
    ppermute x6, starting transfers between devices, shift(): return lax.ppermute(v, axis, [(i, (i + by) % n) for i in range(n)])  19.2 us
    all_gather x1, blocking collectives, per_device(): heads = lax.all_gather(attended, NEAR, axis=1, tiled=True)  17.5 us
    all_to_all x1, starting transfers between devices, per_device(): back_sums = lax.all_to_all(dealt, BOTH, 0, 0, tiled=True)  14.3 us
    all_to_all x1, waiting for transfers between devices, per_device(): lax.all_to_all(partial.reshape(nz, feats, tokens), 'z', 0, 0, tiled=True)  14.1 us
    all_to_all x1, starting transfers between devices, per_device(): lax.all_to_all(partial.reshape(nz, feats, tokens), 'z', 0, 0, tiled=True)  10.1 us
    all_to_all x1, starting transfers between devices, per_device(): lax.all_to_all(turned, 'z', 0, 0, tiled=True)  10 us
  transfers between devices with their start and end apart: 12, of which 6 were waited for; matrix products, arithmetic and copies ran while one was open for 14% of the time, Pallas kernels for 0%

commit v1 on v0

--- a/solution.py
+++ b/solution.py
@@ -131,7 +131,9 @@
     attended = sum(
         ((shift(back[k], "x", -k) if k else back[k]).astype(f32) for k in range(nx))
     ).astype(bf16)
-    heads = lax.all_gather(attended, NEAR, axis=1, tiled=True)
+    heads = jnp.concatenate(
+        lax.all_to_all(jnp.stack([attended] * lax.axis_size(NEAR)), NEAR, 0, 0), axis=1
+    )
     partial = lax.dot_general(
         near_weight, heads, (((1,), (1,)), ((), ())), preferred_element_type=f32
     ).astype(bf16)

time: 231 us -> 259 us (1.12)
  waiting for transfers between devices: 49.4 us -> 94.5 us
  blocking collectives: 46.7 us -> 29.6 us
    all_to_all x1, waiting for transfers between devices: 0.01 us -> 28.4 us  [per_device(): lax.all_to_all(turned, 'z', 0, 0, tiled=True)]
    all_to_all x0 -> x1, waiting for transfers between devices: none -> 18.1 us  [per_device(): lax.all_to_all(jnp.stack([attended] * lax.axis_size(NEAR)), NEAR, 0, 0)]
    all_gather x1 -> x0, blocking collectives: 17.5 us -> none  [per_device(): heads = lax.all_gather(attended, NEAR, axis=1, tiled=True)]
    all_to_all x0 -> x1, starting transfers between devices: none -> 13.4 us  [per_device(): lax.all_to_all(jnp.stack([attended] * lax.axis_size(NEAR)), NEAR, 0, 0)]
    all_to_all x1, starting transfers between devices: 14.3 us -> 6.53 us  [per_device(): back_sums = lax.all_to_all(dealt, BOTH, 0, 0, tiled=True)]
    ppermute x1, waiting for transfers between devices: 0.01 us -> 6.91 us  [swap(): return lax.ppermute(v, axis, [(0, 1), (1, 0)])]
    all_to_all x1, starting transfers between devices: 10.1 us -> 3.63 us  [per_device(): lax.all_to_all(partial.reshape(nz, feats, tokens), 'z', 0, 0, tiled=True)]
    all_gather x1, waiting for transfers between devices: 5.36 us -> 0.02 us  [per_device(): down_all = lax.all_gather(w_down[0], 'x', tiled=True)]
  transfers between devices with their start and end apart: 12 -> 13, of which waited for: 6 -> 7; matrix products, arithmetic and copies ran while one was open for 14% -> 12% of each run, Pallas kernels for 0% -> 0%
where the time goes in v1:
time: 259 us; the launch traced here: 258 us
  waiting for transfers between devices  94.5 us (36%)
  starting transfers between devices  61.4 us (24%)
  local copies, waits for them, and re-layouts  34.3 us (13%)
  blocking collectives  29.6 us (11%)
  matrix products  18.9 us (7%)
  between operations  14 us (5%)
  other arithmetic  5.04 us (2%)
    all_to_all x1, blocking collectives, per_device(): lax.all_to_all(sent.reshape(-1, capacity, feats), BOTH, 0, 0, tiled=True)  29.6 us
    all_to_all x1, waiting for transfers between devices, per_device(): lax.all_to_all(turned, 'z', 0, 0, tiled=True)  28.4 us
    all_to_all x1, waiting for transfers between devices, per_device(): back_sums = lax.all_to_all(dealt, BOTH, 0, 0, tiled=True)  21 us
    ppermute x6, starting transfers between devices, shift(): return lax.ppermute(v, axis, [(i, (i + by) % n) for i in range(n)])  20.2 us
    all_to_all x1, waiting for transfers between devices, per_device(): lax.all_to_all(jnp.stack([attended] * lax.axis_size(NEAR)), NEAR, 0, 0)  18.1 us
    all_to_all x1, starting transfers between devices, per_device(): lax.all_to_all(jnp.stack([attended] * lax.axis_size(NEAR)), NEAR, 0, 0)  13.4 us
    all_to_all x1, waiting for transfers between devices, per_device(): lax.all_to_all(partial.reshape(nz, feats, tokens), 'z', 0, 0, tiled=True)  13 us
    all_to_all x1, starting transfers between devices, per_device(): lax.all_to_all(turned, 'z', 0, 0, tiled=True)  10.1 us
  transfers between devices with their start and end apart: 13, of which 7 were waited for; matrix products, arithmetic and copies ran while one was open for 12% of the time, Pallas kernels for 0%

profile of v1, /device:TPU:1, one launch (start us, length us, event | category | flops | bytes accessed | tf_op | source)
XLA Modules:
  0.0 257.7 jit_solution(4171954217951305614)
XLA Ops:
  6.5 5.7 %fusion.77 = (bf16[1,4096,1,128]{3,2,1,0:T(2,128)(2,1)S(1)}, bf16[1,4096,1,128]{3,2,1,0:T(2,128)(2,1)S(1)}) fusion(bf16[1,4096,2,128]{3,2,1,0:T(2,128)(2,1)} %param.26), kind=kLoop, calls=%fused_computation.122 | loop fusion | bytes 4194304 | tf_op jit(solution)/shard_map/slice | solution.py:117
  15.0 3.9 %collective-permute-start = (bf16[400,128]{1,0:T(8,128)(2,1)S(1)}, bf16[400,128]{1,0:T(8,128)(2,1)S(1)}, u32[]{:S(2)}, u32[]{:S(2)}) collective-permute-start(bf16[400,128]{1,0:T(8,128)(2,1)S(1)} %get-tuple-element.33), channel_id=1, source_target_pairs={{0,64},{64,128},{128,192},{192,0},{1,65},{65,129},{129,193},{193,1... | collective-permute-start | bytes 307208 | tf_op jit(solution)/shard_map/ppermute | solution.py:24
  18.9 4.4 %collective-permute-start.1 = (bf16[400,128]{1,0:T(8,128)(2,1)S(1)}, bf16[400,128]{1,0:T(8,128)(2,1)S(1)}, u32[]{:S(2)}, u32[]{:S(2)}) collective-permute-start(bf16[400,128]{1,0:T(8,128)(2,1)S(1)} %get-tuple-element.33), channel_id=1, source_target_pairs={{0,128},{64,192},{128,0},{192,64},{1,129},{65,193},{129,1},{193,65... | collective-permute-start | bytes 307208 | tf_op jit(solution)/shard_map/ppermute | solution.py:24
  23.3 3.1 %collective-permute-start.2 = (bf16[400,128]{1,0:T(8,128)(2,1)S(1)}, bf16[400,128]{1,0:T(8,128)(2,1)S(1)}, u32[]{:S(2)}, u32[]{:S(2)}) collective-permute-start(bf16[400,128]{1,0:T(8,128)(2,1)S(1)} %get-tuple-element.33), channel_id=1, source_target_pairs={{0,192},{64,0},{128,64},{192,128},{1,193},{65,1},{129,65},{193,129... | collective-permute-start | bytes 307208 | tf_op jit(solution)/shard_map/ppermute | solution.py:24
  27.5 7.5 %collective-permute-start.3 = (bf16[1206,128]{1,0:T(8,128)(2,1)S(1)}, bf16[1206,128]{1,0:T(8,128)(2,1)S(1)}, u32[]{:S(2)}, u32[]{:S(2)}) collective-permute-start(bf16[1206,128]{1,0:T(8,128)(2,1)S(1)} %pad_maximum_fusion.4), channel_id=1, source_target_pairs={{0,256},{256,0},{1,257},{257,1},{2,258},{258,2},{3,259},{259,3},{4... | collective-permute-start | bytes 926216 | tf_op jit(solution)/shard_map/ppermute | solution.py:19
  35.2 6.9 %collective-permute-done.3 = bf16[1206,128]{1,0:T(8,128)(2,1)S(1)} collective-permute-done((bf16[1206,128]{1,0:T(8,128)(2,1)S(1)}, bf16[1206,128]{1,0:T(8,128)(2,1)S(1)}, u32[]{:S(2)}, u32[]{:S(2)}) %collective-permute-start.3) | collective-permute-done | bytes 308768 | tf_op jit(solution)/shard_map/ppermute | solution.py:19
  48.5 3.6 %collective-permute-start.5 = (bf16[384,128]{1,0:T(8,128)(2,1)S(1)}, bf16[384,128]{1,0:T(8,128)(2,1)S(1)}, u32[]{:S(2)}, u32[]{:S(2)}) collective-permute-start(bf16[384,128]{1,0:T(8,128)(2,1)S(1)} %get-tuple-element.29), channel_id=1, source_target_pairs={{0,128},{64,192},{128,0},{192,64},{1,129},{65,193},{129,1},{193,65... | collective-permute-start | bytes 294920 | tf_op jit(solution)/shard_map/ppermute | solution.py:24
  52.2 2.8 %collective-permute-start.6 = (bf16[384,128]{1,0:T(8,128)(2,1)S(1)}, bf16[384,128]{1,0:T(8,128)(2,1)S(1)}, u32[]{:S(2)}, u32[]{:S(2)}) collective-permute-start(bf16[384,128]{1,0:T(8,128)(2,1)S(1)} %get-tuple-element.28), channel_id=1, source_target_pairs={{0,64},{64,128},{128,192},{192,0},{1,65},{65,129},{129,193},{193,1... | collective-permute-start | bytes 294920 | tf_op jit(solution)/shard_map/ppermute | solution.py:24
  55.0 2.6 collective-permute-done.5
  57.5 3.7 %collective-permute-done.6 = bf16[384,128]{1,0:T(8,128)(2,1)S(1)} collective-permute-done((bf16[384,128]{1,0:T(8,128)(2,1)S(1)}, bf16[384,128]{1,0:T(8,128)(2,1)S(1)}, u32[]{:S(2)}, u32[]{:S(2)}) %collective-permute-start.6) | collective-permute-done | bytes 98336 | tf_op jit(solution)/shard_map/ppermute | solution.py:24
  62.4 13.4 %all-to-all-start = ((bf16[8,384,128]{1,2,0:T(8,128)(2,1)}), bf16[8,384,128]{1,2,0:T(8,128)(2,1)S(1)}, u32[]{:S(2)}, u32[]{:S(2)}) async-start(bf16[8,384,128]{1,2,0:T(8,128)(2,1)} %stack.31), calls=%async_computation | async-start | bytes 1572864 | tf_op jit(solution)/shard_map/all_to_all | solution.py:135
  78.0 18.1 %all-to-all-done = bf16[8,384,128]{1,2,0:T(8,128)(2,1)S(1)} async-done(((bf16[8,384,128]{1,2,0:T(8,128)(2,1)}), bf16[8,384,128]{1,2,0:T(8,128)(2,1)S(1)}, u32[]{:S(2)}, u32[]{:S(2)}) %all-to-all-start) | async-done | bytes 786464 | tf_op jit(solution)/shard_map/all_to_all | solution.py:135
  96.0 10.1 %all-to-all-start.1 = ((bf16[8,64,1024]{2,1,0:T(8,128)(2,1)}), bf16[8,64,1024]{2,1,0:T(8,128)(2,1)S(1)}, u32[]{:S(2)}, u32[]{:S(2)}) async-start(bf16[8,64,1024]{2,1,0:T(8,128)(2,1)} %copy.66), calls=%async_computation.1 | async-start | bytes 2097152 | tf_op jit(solution)/shard_map/all_to_all | solution.py:116
  106.9 28.4 %all-to-all-done.1 = bf16[8,64,1024]{2,1,0:T(8,128)(2,1)S(1)} async-done(((bf16[8,64,1024]{2,1,0:T(8,128)(2,1)}), bf16[8,64,1024]{2,1,0:T(8,128)(2,1)S(1)}, u32[]{:S(2)}, u32[]{:S(2)}) %all-to-all-start.1) | async-done | bytes 1048608 | tf_op jit(solution)/shard_map/all_to_all | solution.py:116
  136.9 3.6 %all-to-all-start.2 = ((bf16[8,64,384]{2,1,0:T(8,128)(2,1)}), bf16[8,64,384]{2,1,0:T(8,128)(2,1)S(1)}, u32[]{:S(2)}, u32[]{:S(2)}) async-start(bf16[8,64,384]{2,1,0:T(8,128)(2,1)} %bitcast.12), calls=%async_computation.2 | async-start | bytes 786432 | tf_op jit(solution)/shard_map/all_to_all | solution.py:140
  141.6 13.0 %all-to-all-done.2 = bf16[8,64,384]{2,1,0:T(8,128)(2,1)S(1)} async-done(((bf16[8,64,384]{2,1,0:T(8,128)(2,1)}), bf16[8,64,384]{2,1,0:T(8,128)(2,1)S(1)}, u32[]{:S(2)}, u32[]{:S(2)}) %all-to-all-start.2) | async-done | bytes 393248 | tf_op jit(solution)/shard_map/all_to_all | solution.py:140
  157.2 29.6 %all_to_all.25 = bf16[128,2,1152]{2,1,0:T(2,128)(2,1)} all-to-all(bf16[128,2,1152]{2,1,0:T(2,128)(2,1)S(1)} %reshape.189), channel_id=1, replica_groups=mesh['yh'=2,'x'=4,'z'=8,'yl'=4,'core'=2] {'yh','z','yl','core'}, dimensions={0} | all-to-all | bytes 1179648 | tf_op jit(solution)/shard_map/all_to_all | solution.py:152
  186.9 2.7 %reshape.190 = bf16[128,36,64]{2,1,0:T(8,128)(2,1)S(1)} reshape(bf16[128,2,1152]{2,1,0:T(2,128)(2,1)} %all_to_all.25) | data formatting | bytes 1179648
  189.6 2.9 %copy.77 = bf16[2,64,36,64]{1,0,3,2:T(2,128)(2,1)} copy(bf16[2,64,36,64]{3,2,1,0:T(8,128)(2,1)S(1)} %bitcast.75) | data formatting | bytes 1179648 | tf_op jit(solution)/shard_map/reshape | solution.py:153
  192.5 2.6 %copy.72 = bf16[2,36,64,64]{3,2,1,0:T(8,128)(2,1)S(1)} copy(bf16[2,36,64,64]{2,0,3,1:T(2,128)(2,1)} %bitcast.78) | data formatting | bytes 1179648 | tf_op jit(solution)/shard_map/transpose | solution.py:153
  204.9 3.0 %convolution_convert_fusion = bf16[72,4096]{1,0:T(8,128)(2,1)S(1)} fusion(bf16[1,512,4096]{2,1,0:T(8,128)(2,1)} %all-gather.7.cloned.1.call-done, bf16[72,128]{1,0:T(8,128)(2,1)S(1)} %fusion.33, bf16[72,128]{1,0:T(8,128)(2,1)S(1)} %fusion.32, bf16[72,128]{1,0:T(8,128)(2,1)S(1)} %fusion.31, bf16[72,128]{1,0:T(8,128)(2,1)S(1)} %fusion.30), kind=kOutput, calls=%fused_computation.5 | convolution fusion | flops 302579712 | bytes 4857856 | tf_op jit(solution)/shard_map/dot_general | solution.py:166
  211.3 3.6 %copy.78 = bf16[2,64,36,64]{3,2,1,0:T(8,128)(2,1)S(1)} copy(bf16[2,64,36,64]{1,0,3,2:T(2,128)(2,1)} %bitcast.79) | data formatting | bytes 1179648 | tf_op jit(solution)/shard_map/reshape | solution.py:171
  216.5 6.5 %all-to-all-start.4 = ((bf16[128,2,1152]{2,1,0:T(2,128)(2,1)}), bf16[128,2,1152]{2,1,0:T(2,128)(2,1)S(1)}, u32[]{:S(2)}, u32[]{:S(2)}) async-start(bf16[128,2,1152]{2,1,0:T(2,128)(2,1)} %reshape.191), calls=%async_computation.4 | async-start | bytes 1179648 | tf_op jit(solution)/shard_map/all_to_all | solution.py:173
  223.1 21.0 %all-to-all-done.4 = bf16[128,2,1152]{2,1,0:T(2,128)(2,1)S(1)} async-done(((bf16[128,2,1152]{2,1,0:T(2,128)(2,1)}), bf16[128,2,1152]{2,1,0:T(2,128)(2,1)S(1)}, u32[]{:S(2)}, u32[]{:S(2)}) %all-to-all-start.4) | async-done | bytes 589856 | tf_op jit(solution)/shard_map/all_to_all | solution.py:173
  (100 shorter events, 40.9 us)
Async XLA Ops:
  6.5 19.8 %copy-start = (bf16[3,201,1024]{2,1,0:T(8,128)(2,1)S(1)}, bf16[3,201,1024]{2,1,0:T(8,128)(2,1)}, u32[]{:S(2)}) copy-start(bf16[3,201,1024]{2,1,0:T(8,128)(2,1)} %param.17) | copy-start | bytes 3704836
  6.5 189.7 %all-gather.5.cloned.1.call-start = ((), (), s32[]{:S(2)}) async-start(), calls=%async_computation.5 | async-start | bytes 10485760 | tf_op jit(solution)/shard_map/all_gather | solution.py:118
  14.0 0.7 copy-start.6
  14.0 0.9 copy-start.2
  15.0 20.1 %collective-permute-start = (bf16[400,128]{1,0:T(8,128)(2,1)S(1)}, bf16[400,128]{1,0:T(8,128)(2,1)S(1)}, u32[]{:S(2)}, u32[]{:S(2)}) collective-permute-start(bf16[400,128]{1,0:T(8,128)(2,1)S(1)} %get-tuple-element.33), channel_id=1, source_target_pairs={{0,64},{64,128},{128,192},{192,0},{1,65},{65,129},{129,193},{193,1... | collective-permute-start | bytes 307208 | tf_op jit(solution)/shard_map/ppermute | solution.py:24
  18.9 16.1 %collective-permute-start.1 = (bf16[400,128]{1,0:T(8,128)(2,1)S(1)}, bf16[400,128]{1,0:T(8,128)(2,1)S(1)}, u32[]{:S(2)}, u32[]{:S(2)}) collective-permute-start(bf16[400,128]{1,0:T(8,128)(2,1)S(1)} %get-tuple-element.33), channel_id=1, source_target_pairs={{0,128},{64,192},{128,0},{192,64},{1,129},{65,193},{129,1},{193,65... | collective-permute-start | bytes 307208 | tf_op jit(solution)/shard_map/ppermute | solution.py:24
  23.3 11.8 %collective-permute-start.2 = (bf16[400,128]{1,0:T(8,128)(2,1)S(1)}, bf16[400,128]{1,0:T(8,128)(2,1)S(1)}, u32[]{:S(2)}, u32[]{:S(2)}) collective-permute-start(bf16[400,128]{1,0:T(8,128)(2,1)S(1)} %get-tuple-element.33), channel_id=1, source_target_pairs={{0,192},{64,0},{128,64},{192,128},{1,193},{65,1},{129,65},{193,129... | collective-permute-start | bytes 307208 | tf_op jit(solution)/shard_map/ppermute | solution.py:24
  27.5 14.6 %collective-permute-start.3 = (bf16[1206,128]{1,0:T(8,128)(2,1)S(1)}, bf16[1206,128]{1,0:T(8,128)(2,1)S(1)}, u32[]{:S(2)}, u32[]{:S(2)}) collective-permute-start(bf16[1206,128]{1,0:T(8,128)(2,1)S(1)} %pad_maximum_fusion.4), channel_id=1, source_target_pairs={{0,256},{256,0},{1,257},{257,1},{2,258},{258,2},{3,259},{259,3},{4... | collective-permute-start | bytes 926216 | tf_op jit(solution)/shard_map/ppermute | solution.py:19
  46.0 29.8 %copy-start.1 = (bf16[8192,64]{0,1:T(8,128)(2,1)S(1)}, bf16[8192,64]{0,1:T(8,128)(2,1)}, u32[]{:S(2)}) copy-start(bf16[8192,64]{0,1:T(8,128)(2,1)} %param.22) | copy-start | bytes 3145732
  46.0 8.9 %collective-permute-start.4 = (bf16[384,128]{1,0:T(8,128)(2,1)S(1)}, bf16[384,128]{1,0:T(8,128)(2,1)S(1)}, u32[]{:S(2)}, u32[]{:S(2)}) collective-permute-start(bf16[384,128]{1,0:T(8,128)(2,1)S(1)} %get-tuple-element.27), channel_id=1, source_target_pairs={{0,192},{64,0},{128,64},{192,128},{1,193},{65,1},{129,65},{193,129... | collective-permute-start | bytes 294920 | tf_op jit(solution)/shard_map/ppermute | solution.py:24
  48.5 9.0 %collective-permute-start.5 = (bf16[384,128]{1,0:T(8,128)(2,1)S(1)}, bf16[384,128]{1,0:T(8,128)(2,1)S(1)}, u32[]{:S(2)}, u32[]{:S(2)}) collective-permute-start(bf16[384,128]{1,0:T(8,128)(2,1)S(1)} %get-tuple-element.29), channel_id=1, source_target_pairs={{0,128},{64,192},{128,0},{192,64},{1,129},{65,193},{129,1},{193,65... | collective-permute-start | bytes 294920 | tf_op jit(solution)/shard_map/ppermute | solution.py:24
  52.2 9.0 %collective-permute-start.6 = (bf16[384,128]{1,0:T(8,128)(2,1)S(1)}, bf16[384,128]{1,0:T(8,128)(2,1)S(1)}, u32[]{:S(2)}, u32[]{:S(2)}) collective-permute-start(bf16[384,128]{1,0:T(8,128)(2,1)S(1)} %get-tuple-element.28), channel_id=1, source_target_pairs={{0,64},{64,128},{128,192},{192,0},{1,65},{65,129},{129,193},{193,1... | collective-permute-start | bytes 294920 | tf_op jit(solution)/shard_map/ppermute | solution.py:24
  62.4 33.6 %all-to-all-start = ((bf16[8,384,128]{1,2,0:T(8,128)(2,1)}), bf16[8,384,128]{1,2,0:T(8,128)(2,1)S(1)}, u32[]{:S(2)}, u32[]{:S(2)}) async-start(bf16[8,384,128]{1,2,0:T(8,128)(2,1)} %stack.31), calls=%async_computation | async-start | bytes 1572864 | tf_op jit(solution)/shard_map/all_to_all | solution.py:135
  96.0 39.3 %all-to-all-start.1 = ((bf16[8,64,1024]{2,1,0:T(8,128)(2,1)}), bf16[8,64,1024]{2,1,0:T(8,128)(2,1)S(1)}, u32[]{:S(2)}, u32[]{:S(2)}) async-start(bf16[8,64,1024]{2,1,0:T(8,128)(2,1)} %copy.66), calls=%async_computation.1 | async-start | bytes 2097152 | tf_op jit(solution)/shard_map/all_to_all | solution.py:116
  106.2 98.7 %all-gather.7.cloned.1.call-start = ((), (), s32[]{:S(2)}) async-start(), calls=%async_computation.6 | async-start | bytes 5242880 | tf_op jit(solution)/shard_map/all_gather | solution.py:119
  106.9 33.7 %copy-start.3 = (s32[384,2]{0,1:T(2,128)S(1)}, s32[384,2]{0,1:T(2,128)}, u32[]{:S(2)}) copy-start(s32[384,2]{0,1:T(2,128)} %param.24) | copy-start | bytes 9220
  136.0 5.6 %copy-start.11 = (f32[64]{0:T(128)S(1)}, f32[64]{0:T(128)}, u32[]{:S(2)}) copy-start(f32[64]{0:T(128)} %param.21) | copy-start | bytes 772
  136.0 18.7 %copy-start.8 = (bf16[384,64]{0,1:T(8,128)(2,1)S(1)}, bf16[384,64]{0,1:T(8,128)(2,1)}, u32[]{:S(2)}) copy-start(bf16[384,64]{0,1:T(8,128)(2,1)} %param.15) | copy-start | bytes 147460
  136.9 17.7 %all-to-all-start.2 = ((bf16[8,64,384]{2,1,0:T(8,128)(2,1)}), bf16[8,64,384]{2,1,0:T(8,128)(2,1)S(1)}, u32[]{:S(2)}, u32[]{:S(2)}) async-start(bf16[8,64,384]{2,1,0:T(8,128)(2,1)} %bitcast.12), calls=%async_computation.2 | async-start | bytes 786432 | tf_op jit(solution)/shard_map/all_to_all | solution.py:140
  192.5 3.8 %copy-start.10 = (f32[4096]{0:T(1024)S(1)}, f32[4096]{0:T(1024)}, u32[]{:S(2)}) copy-start(f32[4096]{0:T(1024)} %param.23) | copy-start | bytes 49156
  196.3 7.0 %copy-start.7 = (bf16[32768,128]{1,0:T(8,128)(2,1)S(1)}, bf16[32768,128]{1,0:T(8,128)(2,1)}, u32[]{:S(2)}) copy-start(bf16[32768,128]{1,0:T(8,128)(2,1)} %all-gather.5.cloned.1.call-done) | copy-start | bytes 25165828
  214.9 8.1 %copy-start.4 = (s32[384,2]{0,1:T(2,128)S(1)}, s32[384,2]{0,1:T(2,128)}, u32[]{:S(2)}) copy-start(s32[384,2]{0,1:T(2,128)} %param.25) | copy-start | bytes 9220
  216.5 27.6 %all-to-all-start.4 = ((bf16[128,2,1152]{2,1,0:T(2,128)(2,1)}), bf16[128,2,1152]{2,1,0:T(2,128)(2,1)S(1)}, u32[]{:S(2)}, u32[]{:S(2)}) async-start(bf16[128,2,1152]{2,1,0:T(2,128)(2,1)} %reshape.191), calls=%async_computation.4 | async-start | bytes 1179648 | tf_op jit(solution)/shard_map/all_to_all | solution.py:173
  246.5 2.8 %copy-start.9 = (bf16[384,64]{0,1:T(8,128)(2,1)S(1)}, bf16[384,64]{0,1:T(8,128)(2,1)}, u32[]{:S(2)}) copy-start(bf16[384,64]{0,1:T(8,128)(2,1)} %param.15) | copy-start | bytes 147460
  (1 other events, 0.7 us)
Sparse Core Ops, SparseCore 0:
  14.2 98.1 all-gather.4
  114.5 54.5 all-gather.6
